TPU v7x, 32 devices: a whole 2x2x4 slice. The times are simulated.
32 devices in a mesh: stars: 32 (over z, y, x, core).
Axes of the slice: x: 2, y: 2, z: 4, core: 2. Of those that a mesh axis runs over, the one named last changes fastest.
Arguments:
- positions: float32 [3, 8192], P(None, 'stars')
- velocities: float32 [3, 8192], P(None, 'stars'), may hold values from -3 to 3
- accelerations: float32 [3, 8192], P(None, 'stars'), may hold values from -360 to 360
- jerk_values: float32 [3, 8192], P(None, 'stars'), may hold values from -120 to 120
- masses: float32 [8192], P('stars'), may hold values from 3.6621095e-05 to 0.00036621094
- star_level: int32 [8192], P('stars'), may hold values from 0 to 3, as said below
- list_fine: int32 [16], replicated, may hold values from 0 to 8191, as said below
- list_mid: int32 [32], replicated, may hold values from 0 to 8191, as said below
- list_all: int32 [112], replicated, may hold values from 0 to 8191, as said below
Outputs:
- final_positions: float32 [3, 8192], P(None, 'stars')
- final_velocities: float32 [3, 8192], P(None, 'stars')
- final_accelerations: float32 [3, 8192], P(None, 'stars')
- final_jerks: float32 [3, 8192], P(None, 'stars')
Inputs may be any that keep to these rules, and one draw needn't show every extreme that they name: `star_level`: exactly 16 stars have level 3, 16 level 2, 80 level 1, the rest level 0; the first and the last star have level 3. `list_fine`: the indices of the stars whose star_level is 3, ascending. `list_mid`: the indices of the stars whose star_level is 2 or 3, ascending. `list_all`: the indices of the stars whose star_level is 1, 2 or 3, ascending.
All inputs are finite; a program needn't handle non-finite values.
Results may differ from a plain program's by a relative error of at most 0.0003.
Values sent between devices are 32-bit elements; how exact they have to be, the bound alone decides.
No kernel may reach another device: no remote copies, remote signals or barrier semaphores. Data moves between devices by JAX's collectives and lax.ppermute only.
A program may use at most 64 MiB of HBM per device.

v0:
```python
import math

import jax
import jax.numpy as jnp
from jax import lax
from jax.sharding import PartitionSpec as P

softening = 0.0001
step_unit = 1.0 / 128.0


def elapsed(star_level, count):
    period = jnp.left_shift(jnp.ones_like(star_level), 3 - star_level)
    latest = (count - 1) // period * period
    return (count - latest).astype(jnp.float32) * step_unit


def predict(place, motion, pull, change, elapse):
    moved = place + elapse * (motion + elapse * (0.5 * pull + elapse * change / 6.0))
    sped = motion + elapse * (pull + 0.5 * elapse * change)
    return (moved, sped)


def correct(place, motion, pull, change, pull_new, change_new, elapse):
    square = elapse * elapse
    sped = motion + 0.5 * elapse * (pull + pull_new) + square * (change - change_new) / 12.0
    moved = place + 0.5 * elapse * (motion + sped) + square * (pull - pull_new) / 12.0
    return (moved, sped)


def pair_sums(target_place, target_motion, field_place, field_motion, field_mass):
    apart = [field_place[index][None, :] - target_place[index][:, None] for index in range(3)]
    closing = [field_motion[index][None, :] - target_motion[index][:, None] for index in range(3)]
    distance = apart[0] * apart[0] + apart[1] * apart[1] + apart[2] * apart[2] + softening
    inverse = lax.rsqrt(distance)
    inverse_square = inverse * inverse
    weight = field_mass[None, :] * inverse * inverse_square
    rate = (
        3.0
        * (apart[0] * closing[0] + apart[1] * closing[1] + apart[2] * closing[2])
        * inverse_square
    )
    pull = jnp.stack([jnp.sum(weight * apart[index], axis=1) for index in range(3)])
    change = jnp.stack(
        [jnp.sum(weight * (closing[index] - rate * apart[index]), axis=1) for index in range(3)]
    )
    return (pull, change)


def local_forces(target_place, target_motion, field_place, field_motion, field_mass):
    total = target_place.shape[1]
    width = math.gcd(total, 128)
    half = width // 2
    count = total // width
    blocks_place = target_place.reshape(3, count, width).transpose(1, 0, 2)
    blocks_motion = target_motion.reshape(3, count, width).transpose(1, 0, 2)

    def one_block(pair):
        first = pair_sums(
            pair[0][:, :half], pair[1][:, :half], field_place, field_motion, field_mass
        )
        second = pair_sums(
            pair[0][:, half:], pair[1][:, half:], field_place, field_motion, field_mass
        )
        return (
            jnp.concatenate([first[0], second[0]], axis=1),
            jnp.concatenate([first[1], second[1]], axis=1),
        )

    pull, change = lax.map(one_block, (blocks_place, blocks_motion))
    return (pull.transpose(1, 0, 2).reshape(3, total), change.transpose(1, 0, 2).reshape(3, total))


def owned(rows, start, local_count):
    local = rows - start
    mine = (local >= 0) & (local < local_count)
    return (mine, jnp.where(mine, local, 0), jnp.where(mine, local, local_count))


def body(
    positions,
    velocities,
    accelerations,
    jerk_values,
    masses,
    star_level,
    list_fine,
    list_mid,
    list_all,
):
    local_count = positions.shape[1]
    start = lax.axis_index("stars") * local_count
    plan = (list_fine, list_mid, list_fine, list_all)
    for step in range(4):
        rows = plan[step]
        mine, source, target = owned(rows, start, local_count)
        weight_mine = mine.astype(jnp.float32)
        elapse = elapsed(star_level, step + 1)
        moved, sped = predict(positions, velocities, accelerations, jerk_values, elapse)
        target_place, target_motion = lax.psum(
            (
                jnp.take(moved, source, axis=1) * weight_mine,
                jnp.take(sped, source, axis=1) * weight_mine,
            ),
            "stars",
        )
        part_pull, part_change = local_forces(target_place, target_motion, moved, sped, masses)
        pull_new, change_new = lax.psum((part_pull, part_change), "stars")
        new_place, new_motion = correct(
            jnp.take(positions, source, axis=1),
            jnp.take(velocities, source, axis=1),
            jnp.take(accelerations, source, axis=1),
            jnp.take(jerk_values, source, axis=1),
            pull_new,
            change_new,
            jnp.take(elapse, source),
        )
        positions = positions.at[:, target].set(new_place, mode="drop")
        velocities = velocities.at[:, target].set(new_motion, mode="drop")
        accelerations = accelerations.at[:, target].set(pull_new, mode="drop")
        jerk_values = jerk_values.at[:, target].set(change_new, mode="drop")
    return (positions, velocities, accelerations, jerk_values)


def solution(mesh):
    in_specs = (
        P(None, "stars"),
        P(None, "stars"),
        P(None, "stars"),
        P(None, "stars"),
        P("stars"),
        P("stars"),
        P(),
        P(),
        P(),
    )
    out_specs = (P(None, "stars"), P(None, "stars"), P(None, "stars"), P(None, "stars"))
    return jax.shard_map(body, mesh=mesh, in_specs=in_specs, out_specs=out_specs, check_vma=False)
```

profile of v0, /device:TPU:0, one launch (start us, length us, event | category | flops | bytes accessed | tf_op | source)
XLA Modules:
  0.0 373.2 jit_solution(1489586264018938515)
XLA Ops:
  0.7 0.9 convert_multiply_fusion
  1.6 0.6 copy-done.2
  2.4 0.6 copy-done.5
  3.1 0.6 gather_fusion.5
  3.8 0.6 gather_fusion.7
  4.4 42.1 %all-reduce.7 = (f32[3,16]{0,1:T(8,128)S(1)}, f32[3,16]{0,1:T(8,128)S(1)}) all-reduce(f32[3,16]{0,1:T(8,128)S(1)} %get-tuple-element.390, f32[3,16]{0,1:T(8,128)S(1)} %get-tuple-element.389), channel_id=1, replica_groups=mesh['stars'=32] {'stars'}, use_global_device_ids=true, to_apply=%region_8.11 | all-reduce | flops 96 | bytes 768 | tf_op jit(solution)/shard_map/psum | solution.py:100
  47.1 0.7 copy-done
  48.4 40.3 %all-reduce.6 = (f32[3,16]{0,1:T(8,128)S(1)}, f32[3,16]{0,1:T(8,128)S(1)}) all-reduce(f32[3,16]{0,1:T(8,128)S(1)} %copy.217, f32[3,16]{0,1:T(8,128)S(1)} %copy.220), channel_id=1, replica_groups=mesh['stars'=32] {'stars'}, use_global_device_ids=true, to_apply=%region_7.10 | all-reduce | flops 96 | bytes 768 | tf_op jit(solution)/shard_map/psum | solution.py:108
  88.7 0.7 gather_fusion.2
  89.4 0.7 gather_fusion.14
  90.2 0.6 gather_fusion.3
  90.9 0.6 gather_fusion.4
  91.6 0.6 gather_fusion.6
  92.2 0.8 scatter_custom_fusion.1
  93.2 0.8 scatter_custom_fusion
  94.1 0.7 scatter_custom_fusion.2
  94.9 0.7 scatter_custom_fusion.3
  95.9 0.5 copy-done.6
  96.4 0.6 gather_fusion.13
  97.2 0.6 gather_fusion.11
  97.8 40.2 %all-reduce.5 = (f32[3,32]{0,1:T(8,128)S(1)}, f32[3,32]{0,1:T(8,128)S(1)}) all-reduce(f32[3,32]{0,1:T(8,128)S(1)} %get-tuple-element.386, f32[3,32]{0,1:T(8,128)S(1)} %get-tuple-element.385), channel_id=1, replica_groups=mesh['stars'=32] {'stars'}, use_global_device_ids=true, to_apply=%region_28.32 | all-reduce | flops 192 | bytes 1536 | tf_op jit(solution)/shard_map/psum | solution.py:100
  138.5 0.4 fusion.37
  139.0 40.0 %all-reduce.4 = (f32[3,32]{1,0:T(4,128)S(1)}, f32[3,32]{1,0:T(4,128)S(1)}) all-reduce(f32[3,32]{1,0:T(4,128)S(1)} %maximum_maximum_fusion.2, f32[3,32]{1,0:T(4,128)S(1)} %maximum_maximum_fusion.3), channel_id=1, replica_groups=mesh['stars'=32] {'stars'}, use_global_device_ids=true, to_apply=%region_27.31 | all-reduce | flops 192 | bytes 1536 | tf_op jit(solution)/shard_map/psum | solution.py:108
  179.2 0.6 gather_fusion.10
  179.7 0.8 scatter_fusion.2
  180.7 0.6 gather_fusion.12
  181.3 0.8 scatter_fusion.3
  182.1 0.6 gather_fusion.9
  182.8 0.6 gather_fusion.8
  183.6 0.7 gather_fusion
  184.4 0.7 scatter_fusion.1
  185.3 0.8 scatter_fusion
  186.3 0.6 gather_fusion.19
  187.0 0.6 gather_fusion.17
  187.7 40.2 %all-reduce.3 = (f32[3,16]{0,1:T(8,128)S(1)}, f32[3,16]{0,1:T(8,128)S(1)}) all-reduce(f32[3,16]{0,1:T(8,128)S(1)} %get-tuple-element.382, f32[3,16]{0,1:T(8,128)S(1)} %get-tuple-element.381), channel_id=1, replica_groups=mesh['stars'=32] {'stars'}, use_global_device_ids=true, to_apply=%region_48.52 | all-reduce | flops 96 | bytes 768 | tf_op jit(solution)/shard_map/psum | solution.py:100
  228.3 0.4 fusion.83
  229.1 40.1 %all-reduce.2 = (f32[3,16]{0,1:T(8,128)S(1)}, f32[3,16]{0,1:T(8,128)S(1)}) all-reduce(f32[3,16]{0,1:T(8,128)S(1)} %copy.247, f32[3,16]{0,1:T(8,128)S(1)} %copy.252), channel_id=1, replica_groups=mesh['stars'=32] {'stars'}, use_global_device_ids=true, to_apply=%region_47.51 | all-reduce | flops 96 | bytes 768 | tf_op jit(solution)/shard_map/psum | solution.py:108
  269.2 0.6 gather_fusion.18
  269.8 0.7 scatter_custom_fusion.11
  270.6 0.6 gather_fusion.16
  271.1 0.7 scatter_custom_fusion.10
  271.9 0.6 gather_fusion.15
  272.5 0.8 scatter_custom_fusion.9
  273.4 0.8 scatter_custom_fusion.8
  274.5 0.5 copy-done.7
  275.0 0.6 gather_fusion.23
  275.8 0.6 gather_fusion.24
  276.7 40.7 %all-reduce.1 = (f32[7,3,16]{2,1,0:T(4,128)S(1)}, f32[7,3,16]{2,1,0:T(4,128)S(1)}) all-reduce(f32[7,3,16]{2,1,0:T(4,128)S(1)} %bitcast.434, f32[7,3,16]{2,1,0:T(4,128)S(1)} %bitcast.435), channel_id=1, replica_groups=mesh['stars'=32] {'stars'}, use_global_device_ids=true, to_apply=%region_60.65 | all-reduce | flops 672 | bytes 5376 | tf_op jit(solution)/shard_map/psum | solution.py:100
  317.4 4.7 %while.2 = (s32[]{:T(128)}, f32[7,3,16]{2,1,0:T(4,128)S(1)}, f32[7,3,16]{2,1,0:T(4,128)S(1)}, f32[256]{0:T(256)S(1)}, f32[3,256]{1,0:T(4,128)S(1)}, /*index=5*/f...) while((s32[]{:T(128)}, f32[7,3,16]{2,1,0:T(4,128)S(1)}, ...), condition=%wide.region_75.80_spmd, body=%wide.region_62.79_spmd.sunk | while | flops 164226 | bytes 32105 | solution.py:70
  317.6 0.4 fusion.259
  322.3 40.0 %all-reduce = (f32[3,112]{1,0:T(4,128)S(1)}, f32[3,112]{1,0:T(4,128)S(1)}) all-reduce(f32[3,112]{1,0:T(4,128)S(1)} %reshape.155, f32[3,112]{1,0:T(4,128)S(1)} %reshape.156), channel_id=1, replica_groups=mesh['stars'=32] {'stars'}, use_global_device_ids=true, to_apply=%region_76.81 | all-reduce | flops 672 | bytes 5376 | tf_op jit(solution)/shard_map/psum | solution.py:108
  362.3 0.6 gather_fusion.25
  363.0 0.9 scatter_fusion.7
  363.9 0.7 copy.277
  364.7 0.6 gather_fusion.22
  365.3 0.9 scatter_fusion.6
  366.3 0.7 copy.276
  367.1 0.7 gather_fusion.21
  367.8 0.7 gather_fusion.20
  368.5 1.3 gather_fusion.1
  369.9 0.9 scatter_fusion.5
  370.9 0.7 copy.275
  371.6 0.9 scatter_fusion.4
  372.6 0.7 copy.274
  (161 shorter events, 11.5 us)
Async XLA Ops:
  0.6 1.0 copy-start.3
  0.6 1.0 copy-start.4
  1.5 0.7 copy-start.2
  1.6 0.7 copy-start.1
  2.4 0.7 copy-start.5
  47.1 0.7 copy-start
  95.8 0.7 copy-start.6
  274.3 0.7 copy-start.7
where the time goes:
time: 375 us; the launch traced here: 373 us
  blocking collectives  324 us (86%)
  local copies, waits for them, and re-layouts  38.7 us (10%)
  other arithmetic  9.65 us (3%)
    psum x4, blocking collectives, body(): lax.psum((jnp.take(moved, source, axis=1) * weight_mine, jnp.take(sped, s...  163 us
    psum x4, blocking collectives, body(): pull_new, change_new = lax.psum((part_pull, part_change), 'stars')  160 us

commit v1 on v0

v1 whole, which is shorter than its diff:
```python
import functools

import jax
import jax.numpy as jnp
from jax import lax
from jax.experimental import pallas as pl
from jax.experimental.pallas import tpu as pltpu
from jax.sharding import PartitionSpec as P

softening = 0.0001
unit = 1.0 / 128.0
lanes = 128
vmem = pl.BlockSpec(memory_space=pltpu.VMEM)
smem = pl.BlockSpec(memory_space=pltpu.SMEM)


def predict(place, motion, pull, change, elapse):
    moved = place + elapse * (motion + elapse * (0.5 * pull + elapse * change * (1.0 / 6.0)))
    sped = motion + elapse * (pull + 0.5 * elapse * change)
    return moved, sped


def correct(place, motion, pull, change, pull_new, change_new, elapse):
    square = elapse * elapse * (1.0 / 12.0)
    sped = motion + 0.5 * elapse * (pull + pull_new) + square * (change - change_new)
    moved = place + 0.5 * elapse * (motion + sped) + square * (pull - pull_new)
    return moved, sped


def pack_kernel(place, motion, pull, change, mass, level, out):
    for part, ref in enumerate((place, motion, pull, change)):
        for half in range(2):
            out[part, 4 * half : 4 * half + 3, :] = ref[:, half * lanes : (half + 1) * lanes]
    for half in range(2):
        row = slice(half, half + 1)
        spare = slice(4 * half + 3, 4 * half + 4)
        out[0, spare, :] = jnp.where(level[row, :] <= 1, mass[row, :], 0.0)
        out[1, spare, :] = mass[row, :]
        out[2, spare, :] = jnp.zeros((1, lanes), jnp.float32)
        out[3, spare, :] = jnp.zeros((1, lanes), jnp.float32)


def plan_kernel(own, fine, mid, every, order, meta):
    first = lax.axis_index("stars") * own
    count_fine, count_mid, count_all = fine.shape[0], mid.shape[0], every.shape[0]
    for index in range(count_mid, order.shape[0]):
        order[index] = 0

    def merge(index, seen):
        star = mid[index]
        order[count_fine + index - seen] = star
        same = star == fine[jnp.minimum(seen, count_fine - 1)]
        return seen + same.astype(jnp.int32)

    lax.fori_loop(0, count_mid, merge, jnp.int32(0))
    for index in range(count_fine) if count_fine <= 16 else ():
        order[index] = fine[index]
    if count_fine > 16:

        @pl.loop(0, count_fine)
        def _(index):
            order[index] = fine[index]

    def tally(index, pair):
        star = every[index]
        return (
            pair[0] + (star < first).astype(jnp.int32),
            pair[1] + (star < first + own).astype(jnp.int32),
        )

    low, high = lax.fori_loop(0, count_all, tally, (jnp.int32(0), jnp.int32(0)), unroll=8)
    meta[0] = low
    meta[1] = high - low


def pair_terms(target, field, total):
    apart = [field[index] - target[index] for index in range(3)]
    closing = [field[3 + index] - target[3 + index] for index in range(3)]
    distance = apart[0] * apart[0] + apart[1] * apart[1] + (apart[2] * apart[2] + softening)
    inverse = lax.rsqrt(distance)
    square = inverse * inverse
    weight = field[6] * inverse * square
    dot = apart[0] * closing[0] + apart[1] * closing[1] + apart[2] * closing[2]
    rate = 3.0 * dot * square
    pulled = [weight * apart[index] for index in range(3)]
    return [total[index] + pulled[index] for index in range(3)] + [
        total[3 + index] + (weight * closing[index] - rate * pulled[index]) for index in range(3)
    ]


def main_kernel(
    devices,
    own_count,
    sizes,
    order,
    every,
    meta,
    field,
    own,
    level,
    out_place,
    out_motion,
    out_pull,
    out_change,
    ahead,
    slab,
    table,
    names,
    guess,
    mid_field,
    mid_state,
    mid_names,
    result,
):
    count_fine, count_mid, count_all = sizes
    blocks, blocks_fine = count_mid // 8, count_fine // 8
    groups = mid_field.shape[0]
    sub = lax.broadcasted_iota(jnp.int32, (8, lanes), 0)
    lane = lax.broadcasted_iota(jnp.int32, (8, lanes), 1)

    def spread(column):
        return jnp.broadcast_to(column, (8, lanes))

    def lane_total(value):
        return spread(jnp.sum(value, axis=1, keepdims=True))

    def loop(count, body):
        if count <= 4:
            for index in range(count):
                body(index)
        else:
            pl.loop(0, count)(body)

    def rows8(index):
        return pl.ds(index * 8 if isinstance(index, int) else pl.multiple_of(index * 8, 8), 8)

    def look_ahead(index):
        place, motion, pull, change = [field[pl.ds(index * 32 + 8 * part, 8), :] for part in range(4)]
        for step in range(4):
            moved, sped = predict(place, motion, pull, change, (step + 1) * unit)
            ahead[step, index, 0] = moved
            ahead[step, index, 1] = sped

    @pl.loop(0, devices // 4)
    def _(index):
        for inner in range(4):
            look_ahead(index * 4 + inner)

    def fetch(block):
        name = jnp.zeros((8, lanes), jnp.int32)
        for row in range(8):
            star = order[block * 8 + row]
            base = (star // own_count) * 32 + ((star % own_count) // lanes) * 4
            for part in range(4):
                slab[part, 4 * row : 4 * row + 4, :] = field[pl.ds(base + 8 * part, 4), :]
            name = jnp.where(sub == row, star, name)
        names[rows8(block), :] = name
        hit = (name % lanes) == lane
        for part in range(4):
            for component in range(3):
                value = slab[part, pl.ds(component, 8, stride=4), :]
                table[3 * part + component, rows8(block), :] = lane_total(jnp.where(hit, value, 0.0))
        mass = slab[1, pl.ds(3, 8, stride=4), :]
        table[12, rows8(block), :] = lane_total(jnp.where(hit, mass, 0.0))

    loop(blocks, fetch)

    def turn(ref, group, *at):
        total = jnp.zeros((8, lanes), ref.dtype)
        for inner in range(min(16, blocks)):
            value = ref[(*at, rows8(group * 16 + inner), slice(None))]
            total = total + jnp.where(lane == sub + inner * 8, value, jnp.zeros_like(value))
        return jnp.sum(total, axis=0, keepdims=True)

    def fixed(group):
        mid_field[group, 6:7, :] = turn(table, group, 12)
        found = turn(names, group)
        if blocks * 8 < lanes:
            found = jnp.where(lane[0:1, :] < blocks * 8, found, -1)
        mid_names[group, 0:1, :] = found

    loop(groups, fixed)

    def elapse_of(step, fine):
        return unit * (1 if fine or step % 2 == 0 else 2)

    def guess_block(step, fine, block):
        state = [table[index, rows8(block), :] for index in range(12)]
        elapse = elapse_of(step, fine)
        for index in range(3):
            moved, sped = predict(
                state[index], state[3 + index], state[6 + index], state[9 + index], elapse
            )
            guess[index, rows8(block), :] = moved
            guess[3 + index, rows8(block), :] = sped

    def place_mid(group):
        for index in range(6):
            mid_field[group, index : index + 1, :] = turn(guess, group, index)

    def force(step, targets):
        def add(totals, row):
            return [pair_terms(target, row, total) for target, total in zip(targets, totals)]

        def one(index, totals):
            for half in range(2):
                base = 4 * half
                row = [ahead[step, index, 0, base + k : base + k + 1, :] for k in range(3)]
                row += [ahead[step, index, 1, base + k : base + k + 1, :] for k in range(3)]
                row += [field[pl.ds(index * 32 + base + 3, 1), :]]
                totals = add(totals, row)
            return totals

        def some(index, totals):
            for inner in range(4):
                totals = one(index * 4 + inner, totals)
            return totals

        zero = jnp.zeros((8, lanes), jnp.float32)
        totals = [[zero] * 6 for _ in targets]
        for group in range(groups):
            totals = add(totals, [mid_field[group, k : k + 1, :] for k in range(7)])
        totals = lax.fori_loop(0, devices // 4, some, totals)
        return [[lane_total(value) for value in total] for total in totals]

    for step in range(4):
        loop(blocks_fine, functools.partial(guess_block, step, True))
        loop(blocks - blocks_fine, lambda block: guess_block(step, False, block + blocks_fine))
        loop(groups, place_mid)
        if step == 3:
            break

        def advance(pair, step, fine):
            targets = [
                [guess[index, rows8(2 * pair + side), :] for index in range(6)] for side in range(2)
            ]
            elapse = elapse_of(step, fine)
            for side, total in enumerate(force(step, targets)):
                rows = rows8(2 * pair + side)
                for index in range(3):
                    moved, sped = correct(
                        *[table[3 * part + index, rows, :] for part in range(4)],
                        total[index],
                        total[3 + index],
                        elapse,
                    )
                    table[index, rows, :] = moved
                    table[3 + index, rows, :] = sped
                    table[6 + index, rows, :] = total[index]
                    table[9 + index, rows, :] = total[3 + index]

        loop(blocks_fine // 2, functools.partial(advance, step=step, fine=True))
        if step == 1:
            loop(
                (blocks - blocks_fine) // 2,
                lambda pair: advance(pair + blocks_fine // 2, step=1, fine=False),
            )

    def keep(group):
        for index in range(12):
            mid_state[group, index : index + 1, :] = turn(table, group, index)

    loop(groups, keep)
    first = lax.axis_index("stars") * own_count
    low, count = meta[0], meta[1]
    result[...] = jnp.zeros_like(result)

    @pl.loop(0, (count + 7) // 8)
    def _(block):
        name = jnp.full((8, lanes), -1, jnp.int32)
        for row in range(8):
            at = block * 8 + row
            star = every[jnp.minimum(low + at, count_all - 1)]
            name = jnp.where((sub == row) & (at < count), star, name)
        own_hit = [name == lane + (first + half * lanes) for half in range(2)]
        coarse = [own_hit[half] & (level[half : half + 1, :] == 1) for half in range(2)]
        mid_hit = [name == mid_names[group, 0:1, :] for group in range(groups)]

        def find(part, component):
            total = jnp.zeros((8, lanes), jnp.float32)
            for half in range(2):
                at = 4 * half + component
                total = total + jnp.where(coarse[half], own[part, at : at + 1, :], 0.0)
            for group in range(groups):
                at = 3 * part + component
                total = total + jnp.where(mid_hit[group], mid_state[group, at : at + 1, :], 0.0)
            return lane_total(total)

        total = jnp.zeros((8, lanes), jnp.float32)
        for half in range(2):
            total = total + jnp.where(coarse[half], 4 * unit, 0.0)
        for group in range(groups):
            fine = lane + group * lanes < count_fine
            total = total + jnp.where(mid_hit[group], jnp.where(fine, unit, 2 * unit), 0.0)
        elapse = lane_total(total)

        state = [[find(part, index) for index in range(3)] for part in range(4)]
        pairs = [predict(*[state[part][index] for part in range(4)], elapse) for index in range(3)]
        target = [pair[0] for pair in pairs] + [pair[1] for pair in pairs]
        total = force(3, [target])[0]
        for index in range(3):
            moved, sped = correct(
                *[state[part][index] for part in range(4)], total[index], total[3 + index], elapse
            )
            for part, value in enumerate((moved, sped, total[index], total[3 + index])):
                for half in range(2):
                    result[part, half, index] += jnp.where(own_hit[half], value, 0.0)

    for part, ref in enumerate((out_place, out_motion, out_pull, out_change)):
        for half in range(2):
            changed = level[half : half + 1, :] >= 1
            for index in range(3):
                value = jnp.sum(result[part, half, index], axis=0, keepdims=True)
                at = 4 * half + index
                ref[index : index + 1, half * lanes : (half + 1) * lanes] = jnp.where(
                    changed, value, own[part, at : at + 1, :]
                )


def body(devices, place, motion, pull, change, masses, star_level, fine, mid, every):
    own_count = place.shape[1]
    count_mid = mid.shape[0]
    groups = -(-count_mid // lanes)
    mass = masses.reshape(2, lanes)
    level = star_level.reshape(2, lanes)
    own = pl.pallas_call(
        pack_kernel,
        out_shape=jax.ShapeDtypeStruct((4, 8, lanes), jnp.float32),
        in_specs=[vmem] * 6,
        out_specs=vmem,
        name="pack",
    )(place, motion, pull, change, mass, level)
    whole = lax.all_gather(own.reshape(32, lanes), "stars", tiled=True)
    order, meta = pl.pallas_call(
        functools.partial(plan_kernel, own_count),
        out_shape=(
            jax.ShapeDtypeStruct((count_mid + 8,), jnp.int32),
            jax.ShapeDtypeStruct((2,), jnp.int32),
        ),
        in_specs=[smem] * 3,
        out_specs=(smem, smem),
        name="plan",
    )(fine, mid, every)
    sizes = (fine.shape[0], count_mid, every.shape[0])
    result = jax.ShapeDtypeStruct((3, own_count), jnp.float32)
    return pl.pallas_call(
        functools.partial(main_kernel, devices, own_count, sizes),
        out_shape=(result,) * 4,
        in_specs=[smem] * 3 + [vmem] * 3,
        out_specs=(vmem,) * 4,
        scratch_shapes=[
            pltpu.VMEM((4, devices, 2, 8, lanes), jnp.float32),
            pltpu.VMEM((4, 32, lanes), jnp.float32),
            pltpu.VMEM((13, count_mid, lanes), jnp.float32),
            pltpu.VMEM((count_mid, lanes), jnp.int32),
            pltpu.VMEM((6, count_mid, lanes), jnp.float32),
            pltpu.VMEM((groups, 8, lanes), jnp.float32),
            pltpu.VMEM((groups, 16, lanes), jnp.float32),
            pltpu.VMEM((groups, 8, lanes), jnp.int32),
            pltpu.VMEM((4, 2, 3, 8, lanes), jnp.float32),
        ],
        compiler_params=pltpu.CompilerParams(vmem_limit_bytes=56 * 1024 * 1024),
        name="steps",
    )(order, every, meta, whole, own, level)


def solution(mesh):
    split = P(None, "stars")
    return jax.shard_map(
        functools.partial(body, mesh.shape["stars"]),
        mesh=mesh,
        in_specs=(split,) * 4 + (P("stars"),) * 2 + (P(),) * 3,
        out_specs=(split,) * 4,
        check_vma=False,
    )
```

time: 375 us -> 59.1 us (0.16)
  blocking collectives: 324 us -> 47.5 us
  local copies, waits for them, and re-layouts: 38.7 us -> 0 us
  Pallas kernels: 0 us -> 11 us
  other arithmetic: 9.65 us -> 0 us
    psum x8 -> x0, blocking collectives: 324 us -> none  [the longest x4 163 us: body(): lax.psum((jnp.take(moved, source, axis=1) * weight_mine, jnp.take(sped, s...]
    all_gather x0 -> x1, blocking collectives: none -> 47.5 us  [body(): whole = lax.all_gather(own.reshape(32, lanes), 'stars', tiled=True)]
    gather x34 -> x0, local copies, waits for them, and re-layouts: 16.9 us -> none  [the longest x4 3.33 us: body(): jnp.take(elapse, source)]
    pallas_call x0 -> x3, Pallas kernels: none -> 11 us  [the longest x1 7.78 us: body(): pl.pallas_call(functools.partial(main_kernel, devices, own_count, sizes),...]
    scatter x24 -> x0, local copies, waits for them, and re-layouts: 10.4 us -> none  [the longest x7 3.34 us: body(): jerk_values = jerk_values.at[:, target].set(change_new, mode='drop')]
    unnamed x24 -> x0, local copies, waits for them, and re-layouts: 6.25 us -> none
    reduce_sum x10 -> x0, other arithmetic: 3.93 us -> none  [pair_sums(): jnp.sum(weight * (closing[index] - rate * apart[index]), axis=1)]
where the time goes in v1:
time: 59.1 us; the launch traced here: 59.2 us
  blocking collectives  47.5 us (80%)
  Pallas kernels  11 us (19%)
  between operations  0.64 us (1%)
    all_gather x1, blocking collectives, body(): whole = lax.all_gather(own.reshape(32, lanes), 'stars', tiled=True)  47.5 us
    pallas_call x1, Pallas kernels, body(): pl.pallas_call(functools.partial(main_kernel, devices, own_count, sizes),...  7.78 us
    pallas_call x1, Pallas kernels, body(): pl.pallas_call(functools.partial(plan_kernel, own_count), out_shape=(jax....  1.86 us
    pallas_call x1, Pallas kernels, body(): pl.pallas_call(pack_kernel, out_shape=jax.ShapeDtypeStruct((4, 8, lanes),...  1.37 us

profile of v1, /device:TPU:0, one launch (start us, length us, event | category | flops | bytes accessed | tf_op | source)
XLA Modules:
  0.0 59.2 jit_solution(7700154376909063358)
XLA Ops:
  0.6 1.9 %plan.1 = (s32[40]{0:T(128)}, s32[2]{0:T(128)}) custom-call(s32[16]{0:T(128)} %fine.1, s32[32]{0:T(128)} %mid.1, s32[112]{0:T(128)} %every.3), custom_call_target="tpu_custom_call" | custom-call | tf_op jit(solution)/shard_map/plan/pallas_call | solution.py:334
  2.5 1.4 %pack.1.own = f32[4,8,128]{2,1,0:T(8,128)} custom-call(f32[3,256]{1,0:T(4,128)} %place.1, f32[3,256]{1,0:T(4,128)} %motion.1, f32[3,256]{1,0:T(4,128)} %pull.1, f32[3,256]{1,0:T(4,128)} %change.1, f32[2,128]{1,0:T(2,128)} %bitcast.6, s32[2,128]{1,0:T(2,128)} %bitcast.4), custom_call_target="tpu_custom_call" | custom-call | tf_op jit(solution)/shard_map/pack/pallas_call | solution.py:326
  3.9 47.5 %all_gather.3.field = f32[1024,128]{1,0:T(8,128)} all-gather(f32[32,128]{1,0:T(8,128)} %bitcast.3), channel_id=1, replica_groups=mesh['stars'=32] {'stars'}, dimensions={0}, use_global_device_ids=true | all-gather | bytes 540672 | tf_op jit(solution)/shard_map/all_gather | solution.py:333
  51.4 7.8 %steps.1 = (f32[3,256]{1,0:T(4,128)}, f32[3,256]{1,0:T(4,128)}, f32[3,256]{1,0:T(4,128)}, f32[3,256]{1,0:T(4,128)}) custom-call(s32[40]{0:T(128)} %get-tuple-element.6.order, s32[112]{0:T(128)} %every.3, s32[2]{0:T(128)} %get-tuple-element.7.meta, f32[1024,128]{1,0:T(8,128)} %all_gather.3.field, f32[4,8,128]{2,1,0:T(8,128)} %pack.1.own, s32[2,128]{1,0:T(2,128)} %bitcast.5), custom_call_target="tpu_custom_call" | custom-call | tf_op jit(solution)/shard_map/steps/pallas_call | solution.py:346

commit v2 on v1

--- a/solution.py
+++ b/solution.py
@@ -86,6 +86,38 @@
     return [total[index] + pulled[index] for index in range(3)] + [
         total[3 + index] + (weight * closing[index] - rate * pulled[index]) for index in range(3)
     ]
+
+
+def rounds_of(devices):
+    bits = devices.bit_length() - 1
+    assert devices == 1 << bits
+    rounds = []
+    high = bits
+    while high > 1:
+        width = 1 if (high - 1) % 2 else 2
+        high -= width
+        rounds.append((1 << high, 1 << width))
+    if high == 1:
+        rounds.append((1, 2))
+    return rounds
+
+
+def gather(block, devices):
+    for stride, radix in rounds_of(devices):
+        parts = [block]
+        for turn in range(1, radix):
+            pairs = [(device, device ^ (turn * stride)) for device in range(devices)]
+            parts.append(lax.ppermute(block, "stars", pairs))
+        block = jnp.concatenate(parts, axis=0)
+    return block
+
+
+def slot_of(apart, devices):
+    slot, held = 0, 1
+    for stride, radix in rounds_of(devices):
+        slot = slot + ((apart // stride) % radix) * held
+        held *= radix
+    return slot
 
 
 def main_kernel(
@@ -146,11 +178,13 @@
         for inner in range(4):
             look_ahead(index * 4 + inner)
 
+    me = lax.axis_index("stars")
+
     def fetch(block):
         name = jnp.zeros((8, lanes), jnp.int32)
         for row in range(8):
             star = order[block * 8 + row]
-            base = (star // own_count) * 32 + ((star % own_count) // lanes) * 4
+            base = slot_of((star // own_count) ^ me, devices) * 32 + ((star % own_count) // lanes) * 4
             for part in range(4):
                 slab[part, 4 * row : 4 * row + 4, :] = field[pl.ds(base + 8 * part, 4), :]
             name = jnp.where(sub == row, star, name)
@@ -261,7 +295,7 @@
             mid_state[group, index : index + 1, :] = turn(table, group, index)
 
     loop(groups, keep)
-    first = lax.axis_index("stars") * own_count
+    first = me * own_count
     low, count = meta[0], meta[1]
     result[...] = jnp.zeros_like(result)
 
@@ -330,7 +364,7 @@
         out_specs=vmem,
         name="pack",
     )(place, motion, pull, change, mass, level)
-    whole = lax.all_gather(own.reshape(32, lanes), "stars", tiled=True)
+    whole = gather(own.reshape(32, lanes), devices)
     order, meta = pl.pallas_call(
         functools.partial(plan_kernel, own_count),
         out_shape=(

time: 59.1 us -> 32.3 us (0.55)
  blocking collectives: 47.5 us -> 0 us
  waiting for transfers between devices: 0 us -> 9.6 us
  starting transfers between devices: 0 us -> 9.24 us
  local copies, waits for them, and re-layouts: 0 us -> 1.64 us
    all_gather x1 -> x0, blocking collectives: 47.5 us -> none  [body(): whole = lax.all_gather(own.reshape(32, lanes), 'stars', tiled=True)]
    ppermute x0 -> x7, waiting for transfers between devices: none -> 9.6 us  [gather(): parts.append(lax.ppermute(block, 'stars', pairs))]
    ppermute x0 -> x7, starting transfers between devices: none -> 9.24 us  [gather(): parts.append(lax.ppermute(block, 'stars', pairs))]
    unnamed x0 -> x10, local copies, waits for them, and re-layouts: none -> 1.61 us
  transfers between devices with their start and end apart: 0 -> 7, of which waited for: 0 -> 5; matrix products, arithmetic and copies ran while one was open for 0% -> 3% of each run, Pallas kernels for 0% -> 6%
where the time goes in v2:
time: 32.3 us; the launch traced here: 32 us
  Pallas kernels  10.8 us (33%)
  waiting for transfers between devices  9.6 us (30%)
  starting transfers between devices  9.24 us (29%)
  local copies, waits for them, and re-layouts  1.64 us (5%)
  between operations  0.7 us (2%)
    ppermute x7, waiting for transfers between devices, gather(): parts.append(lax.ppermute(block, 'stars', pairs))  9.6 us
    ppermute x7, starting transfers between devices, gather(): parts.append(lax.ppermute(block, 'stars', pairs))  9.24 us
    pallas_call x1, Pallas kernels, body(): pl.pallas_call(functools.partial(main_kernel, devices, own_count, sizes),...  7.59 us
    pallas_call x1, Pallas kernels, body(): pl.pallas_call(functools.partial(plan_kernel, own_count), out_shape=(jax....  1.86 us
    unnamed x10, local copies, waits for them, and re-layouts  1.61 us
    pallas_call x1, Pallas kernels, body(): pl.pallas_call(pack_kernel, out_shape=jax.ShapeDtypeStruct((4, 8, lanes),...  1.37 us
  transfers between devices with their start and end apart: 7, of which 5 were waited for; matrix products, arithmetic and copies ran while one was open for 3% of the time, Pallas kernels for 6%

profile of v2, /device:TPU:0, one launch (start us, length us, event | category | flops | bytes accessed | tf_op | source)
XLA Modules:
  0.0 32.0 jit_solution(5216201634625616570)
XLA Ops:
  0.6 1.4 %pack.1.own = f32[4,8,128]{2,1,0:T(8,128)} custom-call(f32[3,256]{1,0:T(4,128)} %place.1, f32[3,256]{1,0:T(4,128)} %motion.1, f32[3,256]{1,0:T(4,128)} %pull.1, f32[3,256]{1,0:T(4,128)} %change.1, f32[2,128]{1,0:T(2,128)} %bitcast.11, s32[2,128]{1,0:T(2,128)} %bitcast.9), custom_call_target="tpu_custom_call" | custom-call | tf_op jit(solution)/shard_map/pack/pallas_call | solution.py:360
  2.0 0.0 copy-start.1
  2.0 3.0 %collective-permute-start = (f32[32,128]{1,0:T(8,128)}, f32[32,128]{1,0:T(8,128)S(1)}, u32[]{:S(2)}, u32[]{:S(2)}) collective-permute-start(f32[32,128]{1,0:T(8,128)} %bitcast.5), channel_id=1, source_target_pairs={{0,8},{1,9},{2,10},{3,11},{4,12},{5,13},{6,14},{7,15},{8,0},{9,1},... | collective-permute-start | bytes 49160 | tf_op jit(solution)/shard_map/ppermute | solution.py:110
  5.0 2.6 %collective-permute-start.1 = (f32[32,128]{1,0:T(8,128)}, f32[32,128]{1,0:T(8,128)S(1)}, u32[]{:S(2)}, u32[]{:S(2)}) collective-permute-start(f32[32,128]{1,0:T(8,128)} %bitcast.6), channel_id=1, source_target_pairs={{0,16},{1,17},{2,18},{3,19},{4,20},{5,21},{6,22},{7,23},{8,24},{9,... | collective-permute-start | bytes 49160 | tf_op jit(solution)/shard_map/ppermute | solution.py:110
  7.6 0.0 collective-permute-start.2
  7.6 0.8 %constant_dynamic-update-slice_fusion.6 = (f32[512,128]{1,0:T(8,128)S(1)}, f32[1024,128]{1,0:T(8,128)S(1)}) fusion(f32[4,8,128]{2,1,0:T(8,128)} %pack.1.own), kind=kLoop, calls=%fused_computation.7 | loop fusion | bytes 49152
  8.4 0.0 collective-permute-done
  8.4 1.5 %collective-permute-done.1 = f32[32,128]{1,0:T(8,128)S(1)} collective-permute-done((f32[32,128]{1,0:T(8,128)}, f32[32,128]{1,0:T(8,128)S(1)}, u32[]{:S(2)}, u32[]{:S(2)}) %collective-permute-start.1) | collective-permute-done | bytes 16416 | tf_op jit(solution)/shard_map/ppermute | solution.py:110
  9.9 3.4 %collective-permute-done.2 = f32[32,128]{1,0:T(8,128)S(1)} collective-permute-done((f32[32,128]{1,0:T(8,128)}, f32[32,128]{1,0:T(8,128)S(1)}, u32[]{:S(2)}, u32[]{:S(2)}) %collective-permute-start.2) | collective-permute-done | bytes 16416 | tf_op jit(solution)/shard_map/ppermute | solution.py:110
  13.4 0.0 copy-done.1
  13.4 1.6 %collective-permute-start.3 = (f32[128,128]{1,0:T(8,128)S(1)}, f32[128,128]{1,0:T(8,128)S(1)}, u32[]{:S(2)}, u32[]{:S(2)}) collective-permute-start(f32[128,128]{1,0:T(8,128)S(1)} %pad_maximum_fusion), channel_id=1, source_target_pairs={{0,2},{1,3},{2,0},{3,1},{4,6},{5,7},{6,4},{7,5},{8,10},{9,11},{10,... | collective-permute-start | bytes 196616 | tf_op jit(solution)/shard_map/ppermute | solution.py:110
  14.9 1.5 %collective-permute-start.4 = (f32[128,128]{1,0:T(8,128)S(1)}, f32[128,128]{1,0:T(8,128)S(1)}, u32[]{:S(2)}, u32[]{:S(2)}) collective-permute-start(f32[128,128]{1,0:T(8,128)S(1)} %pad_maximum_fusion), channel_id=1, source_target_pairs={{0,4},{1,5},{2,6},{3,7},{4,0},{5,1},{6,2},{7,3},{8,12},{9,13},{10,... | collective-permute-start | bytes 196616 | tf_op jit(solution)/shard_map/ppermute | solution.py:110
  16.4 0.5 %collective-permute-start.5 = (f32[128,128]{1,0:T(8,128)S(1)}, f32[128,128]{1,0:T(8,128)S(1)}, u32[]{:S(2)}, u32[]{:S(2)}) collective-permute-start(f32[128,128]{1,0:T(8,128)S(1)} %pad_maximum_fusion), channel_id=1, source_target_pairs={{0,6},{1,7},{2,4},{3,5},{4,2},{5,3},{6,0},{7,1},{8,14},{9,15},{10,... | collective-permute-start | bytes 196616 | tf_op jit(solution)/shard_map/ppermute | solution.py:110
  16.9 1.0 %collective-permute-done.3 = f32[128,128]{1,0:T(8,128)S(1)} collective-permute-done((f32[128,128]{1,0:T(8,128)S(1)}, f32[128,128]{1,0:T(8,128)S(1)}, u32[]{:S(2)}, u32[]{:S(2)}) %collective-permute-start.3) | collective-permute-done | bytes 65568 | tf_op jit(solution)/shard_map/ppermute | solution.py:110
  18.0 1.2 %collective-permute-done.4 = f32[128,128]{1,0:T(8,128)S(1)} collective-permute-done((f32[128,128]{1,0:T(8,128)S(1)}, f32[128,128]{1,0:T(8,128)S(1)}, u32[]{:S(2)}, u32[]{:S(2)}) %collective-permute-start.4) | collective-permute-done | bytes 65568 | tf_op jit(solution)/shard_map/ppermute | solution.py:110
  19.2 2.4 %collective-permute-done.5 = f32[128,128]{1,0:T(8,128)S(1)} collective-permute-done((f32[128,128]{1,0:T(8,128)S(1)}, f32[128,128]{1,0:T(8,128)S(1)}, u32[]{:S(2)}, u32[]{:S(2)}) %collective-permute-start.5) | collective-permute-done | bytes 65568 | tf_op jit(solution)/shard_map/ppermute | solution.py:110
  21.6 0.1 collective-permute-start.6
  21.7 1.9 %plan.1 = (s32[40]{0:T(128)}, s32[2]{0:T(128)}) custom-call(s32[16]{0:T(128)} %fine.1, s32[32]{0:T(128)} %mid.1, s32[112]{0:T(128)} %every.3), custom_call_target="tpu_custom_call" | custom-call | tf_op jit(solution)/shard_map/plan/pallas_call | solution.py:368
  23.6 0.0 collective-permute-done.6
  23.6 0.0 copy-start
  23.6 0.8 %copy-done = f32[1024,128]{1,0:T(8,128)} copy-done((f32[1024,128]{1,0:T(8,128)}, f32[1024,128]{1,0:T(8,128)S(1)}, u32[]{:S(2)}) %copy-start) | copy-done | bytes 524312
  24.4 7.6 %steps.1 = (f32[3,256]{1,0:T(4,128)}, f32[3,256]{1,0:T(4,128)}, f32[3,256]{1,0:T(4,128)}, f32[3,256]{1,0:T(4,128)}) custom-call(s32[40]{0:T(128)} %get-tuple-element.6.order, s32[112]{0:T(128)} %every.3, s32[2]{0:T(128)} %get-tuple-element.7.meta, f32[1024,128]{1,0:T(8,128)} %copy-done, f32[4,8,128]{2,1,0:T(8,128)} %pack.1.own, s32[2,128]{1,0:T(2,128)} %bitcast.10), custom_call_target="tpu_custom_call" | custom-call | tf_op jit(solution)/shard_map/steps/pallas_call | solution.py:380
  (8 shorter events, 0.1 us)
Async XLA Ops:
  2.0 11.4 %copy-start.1 = (f32[4,8,128]{2,1,0:T(8,128)S(1)}, f32[4,8,128]{2,1,0:T(8,128)}, u32[]{:S(2)}) copy-start(f32[4,8,128]{2,1,0:T(8,128)} %pack.1.own) | copy-start | bytes 49156
  2.0 6.4 %collective-permute-start = (f32[32,128]{1,0:T(8,128)}, f32[32,128]{1,0:T(8,128)S(1)}, u32[]{:S(2)}, u32[]{:S(2)}) collective-permute-start(f32[32,128]{1,0:T(8,128)} %bitcast.5), channel_id=1, source_target_pairs={{0,8},{1,9},{2,10},{3,11},{4,12},{5,13},{6,14},{7,15},{8,0},{9,1},... | collective-permute-start | bytes 49160 | tf_op jit(solution)/shard_map/ppermute | solution.py:110
  5.0 4.9 %collective-permute-start.1 = (f32[32,128]{1,0:T(8,128)}, f32[32,128]{1,0:T(8,128)S(1)}, u32[]{:S(2)}, u32[]{:S(2)}) collective-permute-start(f32[32,128]{1,0:T(8,128)} %bitcast.6), channel_id=1, source_target_pairs={{0,16},{1,17},{2,18},{3,19},{4,20},{5,21},{6,22},{7,23},{8,24},{9,... | collective-permute-start | bytes 49160 | tf_op jit(solution)/shard_map/ppermute | solution.py:110
  7.6 5.7 %collective-permute-start.2 = (f32[32,128]{1,0:T(8,128)}, f32[32,128]{1,0:T(8,128)S(1)}, u32[]{:S(2)}, u32[]{:S(2)}) collective-permute-start(f32[32,128]{1,0:T(8,128)} %bitcast.7), channel_id=1, source_target_pairs={{0,24},{1,25},{2,26},{3,27},{4,28},{5,29},{6,30},{7,31},{8,16},{9,... | collective-permute-start | bytes 49160 | tf_op jit(solution)/shard_map/ppermute | solution.py:110
  13.4 4.6 %collective-permute-start.3 = (f32[128,128]{1,0:T(8,128)S(1)}, f32[128,128]{1,0:T(8,128)S(1)}, u32[]{:S(2)}, u32[]{:S(2)}) collective-permute-start(f32[128,128]{1,0:T(8,128)S(1)} %pad_maximum_fusion), channel_id=1, source_target_pairs={{0,2},{1,3},{2,0},{3,1},{4,6},{5,7},{6,4},{7,5},{8,10},{9,11},{10,... | collective-permute-start | bytes 196616 | tf_op jit(solution)/shard_map/ppermute | solution.py:110
  14.9 4.3 %collective-permute-start.4 = (f32[128,128]{1,0:T(8,128)S(1)}, f32[128,128]{1,0:T(8,128)S(1)}, u32[]{:S(2)}, u32[]{:S(2)}) collective-permute-start(f32[128,128]{1,0:T(8,128)S(1)} %pad_maximum_fusion), channel_id=1, source_target_pairs={{0,4},{1,5},{2,6},{3,7},{4,0},{5,1},{6,2},{7,3},{8,12},{9,13},{10,... | collective-permute-start | bytes 196616 | tf_op jit(solution)/shard_map/ppermute | solution.py:110
  16.4 5.2 %collective-permute-start.5 = (f32[128,128]{1,0:T(8,128)S(1)}, f32[128,128]{1,0:T(8,128)S(1)}, u32[]{:S(2)}, u32[]{:S(2)}) collective-permute-start(f32[128,128]{1,0:T(8,128)S(1)} %pad_maximum_fusion), channel_id=1, source_target_pairs={{0,6},{1,7},{2,4},{3,5},{4,2},{5,3},{6,0},{7,1},{8,14},{9,15},{10,... | collective-permute-start | bytes 196616 | tf_op jit(solution)/shard_map/ppermute | solution.py:110
  21.6 2.0 %collective-permute-start.6 = (f32[512,128]{1,0:T(8,128)S(1)}, f32[512,128]{1,0:T(8,128)S(1)}, u32[]{:S(2)}, u32[]{:S(2)}) collective-permute-start(f32[512,128]{1,0:T(8,128)S(1)} %get-tuple-element.8), channel_id=1, source_target_pairs={{0,1},{1,0},{2,3},{3,2},{4,5},{5,4},{6,7},{7,6},{8,9},{9,8},{10,11... | collective-permute-start | bytes 786440 | tf_op jit(solution)/shard_map/ppermute | solution.py:110
  23.6 0.8 %copy-start = (f32[1024,128]{1,0:T(8,128)}, f32[1024,128]{1,0:T(8,128)S(1)}, u32[]{:S(2)}) copy-start(f32[1024,128]{1,0:T(8,128)S(1)} %constant_dynamic-update-slice_fusion.7.field) | copy-start | bytes 1572868

commit v3 on v2

--- a/solution.py
+++ b/solution.py
@@ -91,25 +91,19 @@
 def rounds_of(devices):
     bits = devices.bit_length() - 1
     assert devices == 1 << bits
-    rounds = []
-    high = bits
-    while high > 1:
-        width = 1 if (high - 1) % 2 else 2
-        high -= width
-        rounds.append((1 << high, 1 << width))
-    if high == 1:
-        rounds.append((1, 2))
-    return rounds
-
-
-def gather(block, devices):
-    for stride, radix in rounds_of(devices):
+    return [(1 << bit, 2) for bit in reversed(range(bits))]
+
+
+def gather(block, devices, beside):
+    for place, (stride, radix) in enumerate(rounds_of(devices)):
         parts = [block]
         for turn in range(1, radix):
             pairs = [(device, device ^ (turn * stride)) for device in range(devices)]
             parts.append(lax.ppermute(block, "stars", pairs))
         block = jnp.concatenate(parts, axis=0)
-    return block
+        if place == 0:
+            block, beside = lax.optimization_barrier((block, beside))
+    return block, beside
 
 
 def slot_of(apart, devices):
@@ -364,7 +358,6 @@
         out_specs=vmem,
         name="pack",
     )(place, motion, pull, change, mass, level)
-    whole = gather(own.reshape(32, lanes), devices)
     order, meta = pl.pallas_call(
         functools.partial(plan_kernel, own_count),
         out_shape=(
@@ -375,7 +368,9 @@
         out_specs=(smem, smem),
         name="plan",
     )(fine, mid, every)
+    whole, (order, meta) = gather(own.reshape(32, lanes), devices, (order, meta))
     sizes = (fine.shape[0], count_mid, every.shape[0])
+    room = devices * 56 * 1024 + count_mid * 16 * 1024 + 4 * 1024 * 1024
     result = jax.ShapeDtypeStruct((3, own_count), jnp.float32)
     return pl.pallas_call(
         functools.partial(main_kernel, devices, own_count, sizes),
@@ -393,7 +388,7 @@
             pltpu.VMEM((groups, 8, lanes), jnp.int32),
             pltpu.VMEM((4, 2, 3, 8, lanes), jnp.float32),
         ],
-        compiler_params=pltpu.CompilerParams(vmem_limit_bytes=56 * 1024 * 1024),
+        compiler_params=pltpu.CompilerParams(vmem_limit_bytes=room),
         name="steps",
     )(order, every, meta, whole, own, level)
 

time: 32.3 us -> 31.4 us (0.972)
  local copies, waits for them, and re-layouts: 1.64 us -> 0.08 us
  other arithmetic: 0.01 us -> 0.75 us
  waiting for transfers between devices: 9.6 us -> 8.93 us
  starting transfers between devices: 9.24 us -> 9.87 us
    unnamed x10 -> x14, local copies, waits for them, and re-layouts: 1.61 us -> 0.06 us
    concatenate x1 -> x4, other arithmetic: 0.01 us -> 0.75 us  [gather(): block = jnp.concatenate(parts, axis=0)]
    ppermute x7 -> x5, waiting for transfers between devices: 9.6 us -> 8.93 us  [gather(): parts.append(lax.ppermute(block, 'stars', pairs))]
    ppermute x7 -> x5, starting transfers between devices: 9.24 us -> 9.87 us  [gather(): parts.append(lax.ppermute(block, 'stars', pairs))]
  transfers between devices with their start and end apart: 7 -> 5, of which waited for: 5 -> 5; matrix products, arithmetic and copies ran while one was open for 3% -> 0% of each run, Pallas kernels for 6% -> 6%
where the time goes in v3:
time: 31.4 us; the launch traced here: 31.1 us
  Pallas kernels  10.7 us (34%)
  starting transfers between devices  9.87 us (31%)
  waiting for transfers between devices  8.93 us (28%)
  between operations  0.77 us (2%)
  other arithmetic  0.75 us (2%)
    ppermute x5, starting transfers between devices, gather(): parts.append(lax.ppermute(block, 'stars', pairs))  9.87 us
    ppermute x5, waiting for transfers between devices, gather(): parts.append(lax.ppermute(block, 'stars', pairs))  8.93 us
    pallas_call x1, Pallas kernels, body(): pl.pallas_call(functools.partial(main_kernel, devices, own_count, sizes),...  7.45 us
    pallas_call x1, Pallas kernels, body(): pl.pallas_call(functools.partial(plan_kernel, own_count), out_shape=(jax....  1.86 us
    pallas_call x1, Pallas kernels, body(): pl.pallas_call(pack_kernel, out_shape=jax.ShapeDtypeStruct((4, 8, lanes),...  1.38 us
    concatenate x4, other arithmetic, gather(): block = jnp.concatenate(parts, axis=0)  0.75 us
  transfers between devices with their start and end apart: 5, of which 5 were waited for; matrix products, arithmetic and copies ran while one was open for 0% of the time, Pallas kernels for 6%

profile of v3, /device:TPU:0, one launch (start us, length us, event | category | flops | bytes accessed | tf_op | source)
XLA Modules:
  0.0 31.1 jit_solution(14038386541602499056)
XLA Ops:
  0.6 1.4 %pack.1.own = f32[4,8,128]{2,1,0:T(8,128)} custom-call(f32[3,256]{1,0:T(4,128)} %place.1, f32[3,256]{1,0:T(4,128)} %motion.1, f32[3,256]{1,0:T(4,128)} %pull.1, f32[3,256]{1,0:T(4,128)} %change.1, f32[2,128]{1,0:T(2,128)} %bitcast.7, s32[2,128]{1,0:T(2,128)} %bitcast.5), custom_call_target="tpu_custom_call" | custom-call | tf_op jit(solution)/shard_map/pack/pallas_call | solution.py:354
  2.0 4.0 %collective-permute-start = (f32[32,128]{1,0:T(8,128)}, f32[32,128]{1,0:T(8,128)S(1)}, u32[]{:S(2)}, u32[]{:S(2)}) collective-permute-start(f32[32,128]{1,0:T(8,128)} %bitcast.3), channel_id=1, source_target_pairs={{0,16},{1,17},{2,18},{3,19},{4,20},{5,21},{6,22},{7,23},{8,24},{9,... | collective-permute-start | bytes 49160 | tf_op jit(solution)/shard_map/ppermute | solution.py:102
  6.0 1.9 %plan.1 = (s32[40]{0:T(128)}, s32[2]{0:T(128)}) custom-call(s32[16]{0:T(128)} %fine.1, s32[32]{0:T(128)} %mid.1, s32[112]{0:T(128)} %every.3), custom_call_target="tpu_custom_call" | custom-call | tf_op jit(solution)/shard_map/plan/pallas_call | solution.py:361
  7.9 0.1 collective-permute-done
  8.0 0.7 %pad_maximum_fusion.3 = f32[64,128]{1,0:T(8,128)S(1)} fusion(f32[32,128]{1,0:T(8,128)S(1)} %collective-permute-done, f32[32,128]{1,0:T(8,128)} %bitcast.4), kind=kLoop, calls=%fused_computation.3 | loop fusion | flops 8192 | bytes 65536 | tf_op jit(solution)/shard_map/concatenate | solution.py:103
  8.7 1.9 %collective-permute-start.1 = (f32[64,128]{1,0:T(8,128)S(1)}, f32[64,128]{1,0:T(8,128)S(1)}, u32[]{:S(2)}, u32[]{:S(2)}) collective-permute-start(f32[64,128]{1,0:T(8,128)S(1)} %pad_maximum_fusion.3), channel_id=1, source_target_pairs={{0,8},{1,9},{2,10},{3,11},{4,12},{5,13},{6,14},{7,15},{8,0},{9,1},... | collective-permute-start | bytes 98312 | tf_op jit(solution)/shard_map/ppermute | solution.py:102
  10.6 2.0 %collective-permute-done.1 = f32[64,128]{1,0:T(8,128)S(1)} collective-permute-done((f32[64,128]{1,0:T(8,128)S(1)}, f32[64,128]{1,0:T(8,128)S(1)}, u32[]{:S(2)}, u32[]{:S(2)}) %collective-permute-start.1) | collective-permute-done | bytes 32800 | tf_op jit(solution)/shard_map/ppermute | solution.py:102
  12.6 1.9 %collective-permute-start.2 = (f32[128,128]{1,0:T(8,128)S(1)}, f32[128,128]{1,0:T(8,128)S(1)}, u32[]{:S(2)}, u32[]{:S(2)}) collective-permute-start(f32[128,128]{1,0:T(8,128)S(1)} %pad_maximum_fusion.2), channel_id=1, source_target_pairs={{0,4},{1,5},{2,6},{3,7},{4,0},{5,1},{6,2},{7,3},{8,12},{9,13},{10,... | collective-permute-start | bytes 196616 | tf_op jit(solution)/shard_map/ppermute | solution.py:102
  14.5 2.4 %collective-permute-done.2 = f32[128,128]{1,0:T(8,128)S(1)} collective-permute-done((f32[128,128]{1,0:T(8,128)S(1)}, f32[128,128]{1,0:T(8,128)S(1)}, u32[]{:S(2)}, u32[]{:S(2)}) %collective-permute-start.2) | collective-permute-done | bytes 65568 | tf_op jit(solution)/shard_map/ppermute | solution.py:102
  16.9 1.9 %collective-permute-start.3 = (f32[256,128]{1,0:T(8,128)S(1)}, f32[256,128]{1,0:T(8,128)S(1)}, u32[]{:S(2)}, u32[]{:S(2)}) collective-permute-start(f32[256,128]{1,0:T(8,128)S(1)} %pad_maximum_fusion.1), channel_id=1, source_target_pairs={{0,2},{1,3},{2,0},{3,1},{4,6},{5,7},{6,4},{7,5},{8,10},{9,11},{10,... | collective-permute-start | bytes 393224 | tf_op jit(solution)/shard_map/ppermute | solution.py:102
  18.8 3.1 %collective-permute-done.3 = f32[256,128]{1,0:T(8,128)S(1)} collective-permute-done((f32[256,128]{1,0:T(8,128)S(1)}, f32[256,128]{1,0:T(8,128)S(1)}, u32[]{:S(2)}, u32[]{:S(2)}) %collective-permute-start.3) | collective-permute-done | bytes 131104 | tf_op jit(solution)/shard_map/ppermute | solution.py:102
  21.9 0.1 collective-permute-start.4
  22.1 0.0 copy-start
  22.1 0.0 copy-start.1
  22.1 0.0 copy-start.2
  22.1 0.0 copy-start.3
  22.1 0.0 copy-start.4
  22.1 1.4 %collective-permute-done.4 = f32[512,128]{1,0:T(8,128)S(1)} collective-permute-done((f32[512,128]{1,0:T(8,128)S(1)}, f32[512,128]{1,0:T(8,128)S(1)}, u32[]{:S(2)}, u32[]{:S(2)}) %collective-permute-start.4) | collective-permute-done | bytes 262176 | tf_op jit(solution)/shard_map/ppermute | solution.py:102
  23.6 0.0 copy-done
  23.6 0.0 copy-done.1
  23.6 0.0 copy-done.2
  23.6 0.0 copy-done.3
  23.6 0.0 copy-done.4
  23.6 7.5 %steps.1 = (f32[3,256]{1,0:T(4,128)}, f32[3,256]{1,0:T(4,128)}, f32[3,256]{1,0:T(4,128)}, f32[3,256]{1,0:T(4,128)}) custom-call(s32[40]{0:T(128)S(1)} %copy-done.3, s32[112]{0:T(128)S(1)} %copy-done.2, s32[2]{0:T(128)S(1)} %copy-done.4, f32[1024,128]{1,0:T(8,128)S(1)} %constant_dynamic-update-slice_fusion.field, f32[4,8,128]{2,1,0:T(8,128)S(1)} %copy-done, ...), custom_call_target="tpu_custom_call" | custom-call | tf_op jit(solution)/shard_map/steps/pallas_call | solution.py:375
  (8 shorter events, 0.1 us)
Async XLA Ops:
  2.0 6.0 %collective-permute-start = (f32[32,128]{1,0:T(8,128)}, f32[32,128]{1,0:T(8,128)S(1)}, u32[]{:S(2)}, u32[]{:S(2)}) collective-permute-start(f32[32,128]{1,0:T(8,128)} %bitcast.3), channel_id=1, source_target_pairs={{0,16},{1,17},{2,18},{3,19},{4,20},{5,21},{6,22},{7,23},{8,24},{9,... | collective-permute-start | bytes 49160 | tf_op jit(solution)/shard_map/ppermute | solution.py:102
  8.7 3.9 %collective-permute-start.1 = (f32[64,128]{1,0:T(8,128)S(1)}, f32[64,128]{1,0:T(8,128)S(1)}, u32[]{:S(2)}, u32[]{:S(2)}) collective-permute-start(f32[64,128]{1,0:T(8,128)S(1)} %pad_maximum_fusion.3), channel_id=1, source_target_pairs={{0,8},{1,9},{2,10},{3,11},{4,12},{5,13},{6,14},{7,15},{8,0},{9,1},... | collective-permute-start | bytes 98312 | tf_op jit(solution)/shard_map/ppermute | solution.py:102
  12.6 4.3 %collective-permute-start.2 = (f32[128,128]{1,0:T(8,128)S(1)}, f32[128,128]{1,0:T(8,128)S(1)}, u32[]{:S(2)}, u32[]{:S(2)}) collective-permute-start(f32[128,128]{1,0:T(8,128)S(1)} %pad_maximum_fusion.2), channel_id=1, source_target_pairs={{0,4},{1,5},{2,6},{3,7},{4,0},{5,1},{6,2},{7,3},{8,12},{9,13},{10,... | collective-permute-start | bytes 196616 | tf_op jit(solution)/shard_map/ppermute | solution.py:102
  16.9 5.0 %collective-permute-start.3 = (f32[256,128]{1,0:T(8,128)S(1)}, f32[256,128]{1,0:T(8,128)S(1)}, u32[]{:S(2)}, u32[]{:S(2)}) collective-permute-start(f32[256,128]{1,0:T(8,128)S(1)} %pad_maximum_fusion.1), channel_id=1, source_target_pairs={{0,2},{1,3},{2,0},{3,1},{4,6},{5,7},{6,4},{7,5},{8,10},{9,11},{10,... | collective-permute-start | bytes 393224 | tf_op jit(solution)/shard_map/ppermute | solution.py:102
  21.9 1.6 %collective-permute-start.4 = (f32[512,128]{1,0:T(8,128)S(1)}, f32[512,128]{1,0:T(8,128)S(1)}, u32[]{:S(2)}, u32[]{:S(2)}) collective-permute-start(f32[512,128]{1,0:T(8,128)S(1)} %pad_maximum_fusion), channel_id=1, source_target_pairs={{0,1},{1,0},{2,3},{3,2},{4,5},{5,4},{6,7},{7,6},{8,9},{9,8},{10,11... | collective-permute-start | bytes 786440 | tf_op jit(solution)/shard_map/ppermute | solution.py:102
  22.1 1.5 %copy-start = (f32[4,8,128]{2,1,0:T(8,128)S(1)}, f32[4,8,128]{2,1,0:T(8,128)}, u32[]{:S(2)}) copy-start(f32[4,8,128]{2,1,0:T(8,128)} %pack.1.own) | copy-start | bytes 49156
  22.1 1.5 %copy-start.1 = (s32[256]{0:T(256)S(1)}, s32[256]{0:T(256)}, u32[]{:S(2)}) copy-start(s32[256]{0:T(256)} %param.14) | copy-start | bytes 3076
  22.1 1.5 %copy-start.2 = (s32[112]{0:T(128)S(1)}, s32[112]{0:T(128)}, u32[]{:S(2)}) copy-start(s32[112]{0:T(128)} %every.3) | copy-start | bytes 1348
  22.1 1.5 %copy-start.3 = (s32[40]{0:T(128)S(1)}, s32[40]{0:T(128)}, u32[]{:S(2)}) copy-start(s32[40]{0:T(128)} %get-tuple-element.11.order) | copy-start | bytes 484
  22.1 1.5 %copy-start.4 = (s32[2]{0:T(128)S(1)}, s32[2]{0:T(128)}, u32[]{:S(2)}) copy-start(s32[2]{0:T(128)} %get-tuple-element.12.meta) | copy-start | bytes 28

commit v4 on v3

--- a/solution.py
+++ b/solution.py
@@ -91,25 +91,41 @@
 def rounds_of(devices):
     bits = devices.bit_length() - 1
     assert devices == 1 << bits
-    return [(1 << bit, 2) for bit in reversed(range(bits))]
+    rounds = []
+    high = bits
+    while high > 1:
+        width = 1 if (high - 1) % 2 else 2
+        high -= width
+        rounds.append((1 << high, 1 << width))
+    if high == 1:
+        rounds.append((1, 2))
+    return rounds
 
 
 def gather(block, devices, beside):
     for place, (stride, radix) in enumerate(rounds_of(devices)):
-        parts = [block]
-        for turn in range(1, radix):
-            pairs = [(device, device ^ (turn * stride)) for device in range(devices)]
-            parts.append(lax.ppermute(block, "stars", pairs))
-        block = jnp.concatenate(parts, axis=0)
+        if stride == 1:
+            pairs = [(device, device ^ 1) for device in range(devices)]
+            block = jnp.concatenate([block, lax.ppermute(block, "stars", pairs)], axis=0)
+        else:
+            groups = [
+                [base + step * stride for step in range(radix)]
+                for base in range(devices)
+                if (base // stride) % radix == 0
+            ]
+            copies = jnp.broadcast_to(block, (radix,) + block.shape)
+            block = lax.all_to_all(copies, "stars", 0, 0, axis_index_groups=groups)
+            block = block.reshape(-1, lanes)
         if place == 0:
             block, beside = lax.optimization_barrier((block, beside))
     return block, beside
 
 
-def slot_of(apart, devices):
+def slot_of(device, me, devices):
     slot, held = 0, 1
     for stride, radix in rounds_of(devices):
-        slot = slot + ((apart // stride) % radix) * held
+        digit = ((device ^ me) if stride == 1 else device) // stride % radix
+        slot = slot + digit * held
         held *= radix
     return slot
 
@@ -122,7 +138,6 @@
     every,
     meta,
     field,
-    own,
     level,
     out_place,
     out_motion,
@@ -173,12 +188,16 @@
             look_ahead(index * 4 + inner)
 
     me = lax.axis_index("stars")
+    mine = slot_of(me, me, devices) * 32
+
+    def own(part, at):
+        return field[pl.ds(mine + (8 * part + at), 1), :]
 
     def fetch(block):
         name = jnp.zeros((8, lanes), jnp.int32)
         for row in range(8):
             star = order[block * 8 + row]
-            base = slot_of((star // own_count) ^ me, devices) * 32 + ((star % own_count) // lanes) * 4
+            base = slot_of(star // own_count, me, devices) * 32 + ((star % own_count) // lanes) * 4
             for part in range(4):
                 slab[part, 4 * row : 4 * row + 4, :] = field[pl.ds(base + 8 * part, 4), :]
             name = jnp.where(sub == row, star, name)
@@ -308,7 +327,7 @@
             total = jnp.zeros((8, lanes), jnp.float32)
             for half in range(2):
                 at = 4 * half + component
-                total = total + jnp.where(coarse[half], own[part, at : at + 1, :], 0.0)
+                total = total + jnp.where(coarse[half], own(part, at), 0.0)
             for group in range(groups):
                 at = 3 * part + component
                 total = total + jnp.where(mid_hit[group], mid_state[group, at : at + 1, :], 0.0)
@@ -341,7 +360,7 @@
                 value = jnp.sum(result[part, half, index], axis=0, keepdims=True)
                 at = 4 * half + index
                 ref[index : index + 1, half * lanes : (half + 1) * lanes] = jnp.where(
-                    changed, value, own[part, at : at + 1, :]
+                    changed, value, own(part, at)
                 )
 
 
@@ -375,7 +394,7 @@
     return pl.pallas_call(
         functools.partial(main_kernel, devices, own_count, sizes),
         out_shape=(result,) * 4,
-        in_specs=[smem] * 3 + [vmem] * 3,
+        in_specs=[smem] * 3 + [vmem] * 2,
         out_specs=(vmem,) * 4,
         scratch_shapes=[
             pltpu.VMEM((4, devices, 2, 8, lanes), jnp.float32),
@@ -390,7 +409,7 @@
         ],
         compiler_params=pltpu.CompilerParams(vmem_limit_bytes=room),
         name="steps",
-    )(order, every, meta, whole, own, level)
+    )(order, every, meta, whole, level)
 
 
 def solution(mesh):

time: 31.4 us -> 34 us (1.083)
  blocking collectives: 0 us -> 9.24 us
  waiting for transfers between devices: 8.93 us -> 5.4 us
  starting transfers between devices: 9.87 us -> 6.39 us
  local copies, waits for them, and re-layouts: 0.08 us -> 1.37 us
  other arithmetic: 0.75 us -> 0.03 us
    ppermute x5 -> x1, starting transfers between devices: 9.87 us -> 0.07 us  [gather(): lax.ppermute(block, 'stars', pairs)]
    all_to_all x0 -> x1, blocking collectives: none -> 9.24 us  [gather(): block = lax.all_to_all(copies, 'stars', 0, 0, axis_index_groups=groups)]
    ppermute x5 -> x1, waiting for transfers between devices: 8.93 us -> 1.52 us  [gather(): lax.ppermute(block, 'stars', pairs)]
    all_to_all x0 -> x1, starting transfers between devices: none -> 6.32 us  [gather(): block = lax.all_to_all(copies, 'stars', 0, 0, axis_index_groups=groups)]
    all_to_all x0 -> x1, waiting for transfers between devices: none -> 3.88 us  [gather(): block = lax.all_to_all(copies, 'stars', 0, 0, axis_index_groups=groups)]
    broadcast_in_dim x0 -> x2, local copies, waits for them, and re-layouts: none -> 1.36 us  [gather(): copies = jnp.broadcast_to(block, (radix,) + block.shape)]
    concatenate x4 -> x1, other arithmetic: 0.75 us -> 0.03 us  [gather(): jnp.concatenate([block, lax.ppermute(block, 'stars', pairs)], axis=0)]
  transfers between devices with their start and end apart: 5 -> 2, of which waited for: 5 -> 2; matrix products, arithmetic and copies ran while one was open for 0% -> 0% of each run, Pallas kernels for 6% -> 6%
where the time goes in v4:
time: 34 us; the launch traced here: 33.5 us
  Pallas kernels  10.4 us (31%)
  blocking collectives  9.24 us (27%)
  starting transfers between devices  6.39 us (19%)
  waiting for transfers between devices  5.4 us (16%)
  local copies, waits for them, and re-layouts  1.37 us (4%)
  between operations  0.69 us (2%)
    all_to_all x1, blocking collectives, gather(): block = lax.all_to_all(copies, 'stars', 0, 0, axis_index_groups=groups)  9.24 us
    pallas_call x1, Pallas kernels, body(): pl.pallas_call(functools.partial(main_kernel, devices, own_count, sizes),...  7.15 us
    all_to_all x1, starting transfers between devices, gather(): block = lax.all_to_all(copies, 'stars', 0, 0, axis_index_groups=groups)  6.32 us
    all_to_all x1, waiting for transfers between devices, gather(): block = lax.all_to_all(copies, 'stars', 0, 0, axis_index_groups=groups)  3.88 us
    pallas_call x1, Pallas kernels, body(): pl.pallas_call(functools.partial(plan_kernel, own_count), out_shape=(jax....  1.86 us
    ppermute x1, waiting for transfers between devices, gather(): lax.ppermute(block, 'stars', pairs)  1.52 us
    pallas_call x1, Pallas kernels, body(): pl.pallas_call(pack_kernel, out_shape=jax.ShapeDtypeStruct((4, 8, lanes),...  1.37 us
    broadcast_in_dim x2, local copies, waits for them, and re-layouts, gather(): copies = jnp.broadcast_to(block, (radix,) + block.shape)  1.36 us
  transfers between devices with their start and end apart: 2, of which 2 were waited for; matrix products, arithmetic and copies ran while one was open for 0% of the time, Pallas kernels for 6%

profile of v4, /device:TPU:0, one launch (start us, length us, event | category | flops | bytes accessed | tf_op | source)
XLA Modules:
  0.0 33.5 jit_solution(8750128337568451136)
XLA Ops:
  0.6 1.4 %pack.1 = f32[4,8,128]{2,1,0:T(8,128)} custom-call(f32[3,256]{1,0:T(4,128)} %place.1, f32[3,256]{1,0:T(4,128)} %motion.1, f32[3,256]{1,0:T(4,128)} %pull.1, f32[3,256]{1,0:T(4,128)} %change.1, f32[2,128]{1,0:T(2,128)} %bitcast.11, s32[2,128]{1,0:T(2,128)} %bitcast.5), custom_call_target="tpu_custom_call" | custom-call | tf_op jit(solution)/shard_map/pack/pallas_call | solution.py:373
  2.0 1.3 %broadcast_in_dim.6 = f32[4,32,128]{2,1,0:T(8,128)} broadcast(f32[32,128]{1,0:T(8,128)} %bitcast.10), dimensions={1,2} | broadcast | bytes 81920 | tf_op jit(solution)/shard_map/broadcast_in_dim | solution.py:116
  3.3 6.3 %all-to-all-start = ((f32[4,32,128]{2,1,0:T(8,128)}), f32[4,32,128]{2,1,0:T(8,128)S(1)}, u32[]{:S(2)}, u32[]{:S(2)}) async-start(f32[4,32,128]{2,1,0:T(8,128)} %broadcast_in_dim.6), calls=%async_computation | async-start | bytes 131072 | tf_op jit(solution)/shard_map/all_to_all | solution.py:117
  9.7 1.9 %plan.1 = (s32[40]{0:T(128)}, s32[2]{0:T(128)}) custom-call(s32[16]{0:T(128)} %fine.1, s32[32]{0:T(128)} %mid.1, s32[112]{0:T(128)} %every.3), custom_call_target="tpu_custom_call" | custom-call | tf_op jit(solution)/shard_map/plan/pallas_call | solution.py:380
  11.5 3.9 %all-to-all-done = f32[4,32,128]{2,1,0:T(8,128)S(1)} async-done(((f32[4,32,128]{2,1,0:T(8,128)}), f32[4,32,128]{2,1,0:T(8,128)S(1)}, u32[]{:S(2)}, u32[]{:S(2)}) %all-to-all-start) | async-done | bytes 65568 | tf_op jit(solution)/shard_map/all_to_all | solution.py:117
  15.4 9.2 %all_to_all.10 = f32[4,128,128]{2,1,0:T(8,128)S(1)} all-to-all(f32[4,128,128]{2,1,0:T(8,128)S(1)} %broadcast_in_dim.7), channel_id=1, replica_groups={{0,2,4,6},{1,3,5,7},{8,10,12,14},{9,11,13,15},{16,18,20,22},{17,19,21,2..., dimensions={0} | all-to-all | bytes 524288 | tf_op jit(solution)/shard_map/all_to_all | solution.py:117
  24.7 0.0 copy-start
  24.7 0.0 copy-start.1
  24.7 0.0 copy-start.2
  24.7 0.0 copy-start.3
  24.7 0.1 collective-permute-start
  24.8 1.5 %collective-permute-done = f32[512,128]{1,0:T(8,128)S(1)} collective-permute-done((f32[512,128]{1,0:T(8,128)S(1)}, f32[512,128]{1,0:T(8,128)S(1)}, u32[]{:S(2)}, u32[]{:S(2)}) %collective-permute-start) | collective-permute-done | bytes 262176 | tf_op jit(solution)/shard_map/ppermute | solution.py:109
  26.3 0.0 copy-done
  26.3 0.0 copy-done.1
  26.3 0.0 copy-done.2
  26.3 0.0 copy-done.3
  26.4 7.2 %steps.1 = (f32[3,256]{1,0:T(4,128)}, f32[3,256]{1,0:T(4,128)}, f32[3,256]{1,0:T(4,128)}, f32[3,256]{1,0:T(4,128)}) custom-call(s32[40]{0:T(128)S(1)} %copy-done.2, s32[112]{0:T(128)S(1)} %copy-done.1, s32[2]{0:T(128)S(1)} %copy-done.3, f32[1024,128]{1,0:T(8,128)S(1)} %pad_maximum_fusion.field, s32[2,128]{1,0:T(2,128)S(1)} %bitcast.6), custom_call_target="tpu_custom_call" | custom-call | tf_op jit(solution)/shard_map/steps/pallas_call | solution.py:394
  (2 shorter events, 0.1 us)
Async XLA Ops:
  3.3 12.1 %all-to-all-start = ((f32[4,32,128]{2,1,0:T(8,128)}), f32[4,32,128]{2,1,0:T(8,128)S(1)}, u32[]{:S(2)}, u32[]{:S(2)}) async-start(f32[4,32,128]{2,1,0:T(8,128)} %broadcast_in_dim.6), calls=%async_computation | async-start | bytes 131072 | tf_op jit(solution)/shard_map/all_to_all | solution.py:117
  24.7 1.7 %copy-start = (s32[256]{0:T(256)S(1)}, s32[256]{0:T(256)}, u32[]{:S(2)}) copy-start(s32[256]{0:T(256)} %param.14) | copy-start | bytes 3076
  24.7 1.7 %copy-start.1 = (s32[112]{0:T(128)S(1)}, s32[112]{0:T(128)}, u32[]{:S(2)}) copy-start(s32[112]{0:T(128)} %every.3) | copy-start | bytes 1348
  24.7 1.7 %copy-start.2 = (s32[40]{0:T(128)S(1)}, s32[40]{0:T(128)}, u32[]{:S(2)}) copy-start(s32[40]{0:T(128)} %get-tuple-element.11.order) | copy-start | bytes 484
  24.7 1.7 %copy-start.3 = (s32[2]{0:T(128)S(1)}, s32[2]{0:T(128)}, u32[]{:S(2)}) copy-start(s32[2]{0:T(128)} %get-tuple-element.12.meta) | copy-start | bytes 28
  24.7 1.6 %collective-permute-start = (f32[512,128]{1,0:T(8,128)S(1)}, f32[512,128]{1,0:T(8,128)S(1)}, u32[]{:S(2)}, u32[]{:S(2)}) collective-permute-start(f32[512,128]{1,0:T(8,128)S(1)} %bitcast.7), channel_id=1, source_target_pairs={{0,1},{1,0},{2,3},{3,2},{4,5},{5,4},{6,7},{7,6},{8,9},{9,8},{10,11... | collective-permute-start | bytes 786440 | tf_op jit(solution)/shard_map/ppermute | solution.py:109
